TPU v7x, 1024 devices: a whole 8x8x8 slice. The times are simulated.
1024 devices in a mesh: row: 128 (over z, x, core), col: 8 (over y).
Axes of the slice: x: 8, y: 8, z: 8, core: 2. Of those that a mesh axis runs over, the one named last changes fastest.
Arguments:
- velocity: float32 [8, 128, 7, 3, 4096], P('col', 'row'), may hold values from -6 to 6
- counts: int32 [8, 128], P('col', 'row'), may hold values from 1 to 7, as said below
Outputs:
- compressive: float32 [8, 128, 7, 3, 4096], P('col', 'row')
- solenoidal: float32 [8, 128, 7, 3, 4096], P('col', 'row')
Inputs may be any that keep to these rules, and one draw needn't show every extreme that they name: In every column c, owners 2t and 2t+1 hold 8 blocks together: counts[c, 2t] + counts[c, 2t+1] = 8. 7 is reached in every column.
All inputs are finite; a program needn't handle non-finite values.
Results may differ from a plain program's by a relative error of at most 0.000096.
Values sent between devices are 32-bit elements; how exact they have to be, the bound alone decides.
A program may use at most 64 MiB of HBM per device.

v0:
```python
import jax
import jax.numpy as jnp
import ml_dtypes
import numpy as np
from jax import lax
from jax.experimental import pallas as pl
from jax.experimental.pallas import tpu as pltpu
from jax.sharding import PartitionSpec as P

MESH = pl.DeviceIdType.MESH
SLOTS = 7
N = 256
F32 = jnp.float32
BF16 = jnp.bfloat16


def split_np(table):
    head = table.astype(ml_dtypes.bfloat16)
    rest = (table - head.astype(np.float64)).astype(ml_dtypes.bfloat16)
    return head, rest


def weights():
    at = np.arange(N)
    angle = 2 * np.pi * ((at[:, None] * at[None, :]) % N) / N
    cos, sin = np.cos(angle), np.sin(angle)
    e_lo, e_hi, py, j0 = np.meshgrid(np.arange(8), np.arange(2), np.arange(8), np.arange(2), indexing="ij")
    y_of = (32 * py + 16 * j0 + 8 * e_hi + e_lo).reshape(-1)
    real_rows, imag_rows = cos[:128], -sin[:128].copy()
    imag_rows[0] = cos[128]
    forward = np.stack([real_rows.reshape(16, 8, N), imag_rows.reshape(16, 8, N)], axis=1).reshape(N, N)
    gain = np.full((128, 1), 2.0)
    gain[0] = 1.0
    back = np.stack([(gain * real_rows).reshape(16, 8, N), (gain * imag_rows).reshape(16, 8, N)], axis=1).reshape(N, N)
    back = back.T / float(N) ** 3
    both = np.concatenate([cos, sin], axis=1)
    return (*split_np(both), *split_np(forward[:, y_of]), *split_np(back[y_of]))


def lane_roll(value, shift):
    return pltpu.roll(value, shift % 128, value.ndim - 1)


def lane_bit(shape, bit):
    return (lax.broadcasted_iota(jnp.int32, shape, len(shape) - 1) // (1 << bit)) % 2 == 1


def swap_bit(low, high, bit):
    upper = lane_bit(low.shape, bit)
    step = 1 << bit
    return jnp.where(upper, lane_roll(high, step), low), jnp.where(upper, high, lane_roll(low, -step))


def swap_bits(items, pairs):
    items = list(items)
    for index_bit, bit in pairs:
        for at in range(len(items)):
            if not (at >> index_bit) & 1:
                other = at | (1 << index_bit)
                items[at], items[other] = swap_bit(items[at], items[other], bit)
    return items


def halves(value):
    head = value.astype(BF16)
    return head, (value - head.astype(F32)).astype(BF16)


def dot(left, right):
    return lax.dot_general(left, right, (((1,), (0,)), ((), ())), preferred_element_type=F32)


def dot_left(head, rest, value):
    value_head, value_rest = halves(value)
    return dot(head, value_head) + (dot(head, value_rest) + dot(rest, value_head))


def dot_right(value, head, rest):
    value_head, value_rest = halves(value)
    return dot(value_head, head) + (dot(value_rest, head) + dot(value_head, rest))


def signed(index):
    return jnp.where(index == N // 2, 0, jnp.where(index > N // 2, index - N, index)).astype(F32)


def spread(number):
    return (number & 1) + 2 * (number & 2) + 4 * (number & 4) + 8 * (number & 8)


def gathered_bits(number):
    return (number & 1) + ((number >> 1) & 2) + ((number >> 2) & 4) + ((number >> 3) & 8)


def stage_y(r1, s2, wy_h, wy_l):
    def lines(d):
        return [
            jnp.concatenate([r1[d, pl.ds(2 * a + e, 16, stride=8), :] for e in range(2)], axis=0) for a in range(4)
        ]

    pair = swap_bits(lines(0) + lines(1), [(0, 4), (1, 5), (2, 6)])
    lone = swap_bits(lines(2), [(0, 4), (1, 5)])
    turned = [lane_roll(item, 64) for item in lone]
    upper = lane_bit((32, 128), 6)
    lone = [jnp.where(upper, b, a) for a, b in zip(lone, turned)] + [jnp.where(upper, a, b) for a, b in zip(lone, turned)]
    both = jnp.concatenate([jnp.concatenate(pair, axis=0), jnp.concatenate(lone, axis=0)], axis=1)
    out = dot_left(wy_h[...], wy_l[...], both)
    s2[:, 0:16, :] = out[:, :128].reshape(16, 16, 128)
    last = out[:, 128:].reshape(16, 2, 8, 128)
    s2[:, 16:24, :] = jnp.where(lane_bit((16, 8, 128), 6), last[:, 1], last[:, 0])


def stage_z(r2, s3, cs_h, cs_l, wave_y):
    tiles = []
    for high in range(2):
        items = [r2[8 * high + low] for low in range(8)]
        tiles.append(swap_bits(items, [(0, 4), (1, 5), (2, 6)]))
    left = jnp.concatenate([jnp.concatenate([tiles[0][i], tiles[1][i]], axis=1) for i in range(8)], axis=0)
    out = dot_right(left, cs_h[...], cs_l[...]).reshape(8, 3, 8, 512)
    by_cos, by_sin = out[..., :256], out[..., 256:]
    kz = lax.broadcasted_iota(jnp.int32, (8, 256), 1)
    wave_z = signed(kz)
    wy = wave_y(lax.broadcasted_iota(jnp.int32, (8, 256), 0))
    for a in range(4):
        first = (by_cos[a, 0] + by_sin[a, 1], by_cos[a, 1] - by_sin[a, 0])
        b = 4 + a
        second = (by_cos[b, 0] + by_sin[b, 1], by_cos[b, 1] - by_sin[b, 0])
        third = (by_cos[a, 2] + by_sin[b, 2], by_cos[b, 2] - by_sin[a, 2])
        rest = tuple(wy * second[i] + wave_z * third[i] for i in range(2))
        for h in range(2):
            lanes = slice(128 * h, 128 * h + 128)
            items = [first[0][:, lanes], first[1][:, lanes], rest[0][:, lanes], rest[1][:, lanes]]
            items = swap_bits(items, [(0, 5), (1, 6)])
            for q in range(4):
                s3[pl.ds((4 * h + q) * 32 + a, 8, stride=4), :] = items[q]


def stage_x(r3, s4, cs_h, cs_l, ky, kz_high):
    shape = (N, 128)
    lane = lax.broadcasted_iota(jnp.int32, shape, 1)
    kx = lax.broadcasted_iota(jnp.int32, shape, 0)
    imag = lane_bit(shape, 5)
    value = r3[...]
    turned = jnp.where(imag, -lane_roll(value, 32), lane_roll(value, -32))
    out = dot_left(cs_h[...], cs_l[...], jnp.concatenate([value, turned], axis=0))
    wave_x = signed(kx)
    wave_z = signed(32 * kz_high + lane % 32)
    wave_y = ky.astype(F32)
    square_sum = jnp.maximum(wave_x * wave_x + wave_y * wave_y + wave_z * wave_z, 1.0)
    factor = jnp.where(lane_bit(shape, 6), 1.0, wave_x)
    terms = factor * out
    fields = (terms + lane_roll(terms, 64)) / square_sum * factor
    turned = jnp.where(imag, lane_roll(fields, 32), -lane_roll(fields, -32))
    s4[...] = dot_left(cs_h[...], cs_l[...], jnp.concatenate([fields, turned], axis=0))


def stage_z_back(r4, s5, cs_h, cs_l, wave_y):
    wave_z = signed(lax.broadcasted_iota(jnp.int32, (8, 256), 1))
    wy = wave_y(lax.broadcasted_iota(jnp.int32, (8, 256), 0))
    rows = [None] * 8
    for a in range(4):
        sides = []
        for h in range(2):
            items = [r4[pl.ds((4 * h + q) * 32 + a, 8, stride=4), :] for q in range(4)]
            sides.append(swap_bits(items, [(0, 5), (1, 6)]))
        first = [jnp.concatenate([sides[0][i], sides[1][i]], axis=1) for i in range(2)]
        pot = [jnp.concatenate([sides[0][2 + i], sides[1][2 + i]], axis=1) for i in range(2)]
        rows[a] = jnp.concatenate([first[0], first[1], wave_z * pot[0]], axis=0)
        rows[4 + a] = jnp.concatenate([wy * pot[0], wy * pot[1], wave_z * pot[1]], axis=0)
    out = dot_right(jnp.concatenate(rows, axis=0), cs_h[...], cs_l[...]).reshape(8, 3, 8, 512)
    by_cos, by_sin = out[..., :256], out[..., 256:]
    items = [None] * 8
    for a in range(4):
        b = 4 + a
        items[a] = jnp.concatenate(
            [by_cos[a, 0] - by_sin[a, 1], by_cos[a, 1] + by_sin[a, 0], by_cos[a, 2] - by_sin[b, 2]], axis=0
        )
        items[b] = jnp.concatenate(
            [by_cos[b, 0] - by_sin[b, 1], by_cos[b, 1] + by_sin[b, 0], by_cos[b, 2] + by_sin[a, 2]], axis=0
        )
    for high in range(2):
        tile = swap_bits([item[:, 128 * high : 128 * high + 128] for item in items], [(0, 4), (1, 5), (2, 6)])
        for low in range(8):
            s5[8 * high + low] = tile[low]


def stage_y_back(r5, s6, vy_h, vy_l):
    pair = r5[:, 0:16, :].reshape(N, 128)
    last = r5[:, 16:24, :]
    last = jnp.stack([last, lane_roll(last, 64)], axis=1).reshape(N, 128)
    out = dot_left(vy_h[...], vy_l[...], jnp.concatenate([pair, last], axis=1))
    pair = swap_bits([out[32 * i : 32 * i + 32, :128] for i in range(8)], [(0, 4), (1, 5), (2, 6)])
    last = [out[32 * i : 32 * i + 32, 128:] for i in range(8)]
    upper = lane_bit((32, 128), 6)
    last = swap_bits([jnp.where(upper, lane_roll(last[4 + i], 64), last[i]) for i in range(4)], [(0, 4), (1, 5)])
    for d, items in enumerate((pair[:4], pair[4:], last)):
        for a in range(4):
            for e in range(2):
                s6[d, pl.ds(2 * a + e, 16, stride=8), :] = items[a][16 * e : 16 * e + 16]


def kernel(
    vel, cnt, cs_h, cs_l, wy_h, wy_l, vy_h, vy_l, comp, sol,
    s0, r0, s1, r1, s2, r2, s3, r3, s4, r4, s5, r5, s6, r6, cb, r7, send, recv,
):
    row, col = lax.axis_index("row"), lax.axis_index("col")
    core = row & 1
    j1, a_hi = col & 1, col >> 1
    px, pz = gathered_bits(row), gathered_bits(row >> 1)
    xi = 4 * px + a_hi
    zi = 2 * pz + j1

    def peer_x(step):
        return (row ^ spread(step >> 2), col ^ (2 * (step & 3)))

    def peer_z(step):
        return (row ^ (2 * spread(step >> 1)), col ^ (step & 1))

    def peer_y(step):
        return (row, col ^ step)

    partner = (row ^ 1, col)

    barrier = pltpu.get_barrier_semaphore()
    for peer, count in ((peer_y, 8), (peer_z, 16), (peer_x, 64)):

        @pl.loop(1, count)
        def _(step, peer=peer):
            pl.semaphore_signal(barrier, inc=1, device_id=peer(step), device_id_type=MESH)

    pl.semaphore_wait(barrier, 7 + 15 + 63)

    def put(source, target, phase, device):
        pltpu.make_async_remote_copy(
            src_ref=source, dst_ref=target, send_sem=send.at[phase], recv_sem=recv.at[phase],
            device_id=device, device_id_type=MESH,
        ).start()

    def keep(source, target, phase):
        pltpu.make_async_copy(source, target, recv.at[phase]).start()

    def arrived(buffer, phase):
        pltpu.make_async_copy(buffer, buffer, recv.at[phase]).wait()

    def left(part, phase):
        pltpu.make_async_copy(part, part, send.at[phase]).wait()

    count = cnt[0, 0]
    for i in range(3):
        s0[i] = vel[jnp.where(core == 1, jnp.maximum(count - 7 + i, 0), 4 + i)]
    put(s0, r0, 0, partner)
    arrived(r0, 0)
    for j in range(4):
        slot = jnp.where(core == 1, count - 4 + j, j)
        owned = jnp.where(core == 1, slot >= 0, j < count)
        mine = vel[jnp.clip(slot, 0, SLOTS - 1)]
        theirs = r0[jnp.clip(jnp.where(core == 1, j, j - 1), 0, 2)]
        block = jnp.where(owned, mine, theirs)
        for d in range(3):
            for quad in range(4):
                at = (2 * quad + j // 2) * 16 + (j % 2) * 8
                s1[d, at : at + 8, :] = block[d, 8 * quad : 8 * quad + 8]

    def exchange_y(source, target, phase):
        for d in range(3):

            @pl.loop(1, 8)
            def _(step, d=d):
                there = pl.multiple_of(16 * (col ^ step), 16)
                here = pl.multiple_of(16 * col, 16)
                put(source.at[d, pl.ds(there, 16)], target.at[d, pl.ds(here, 16)], phase, peer_y(step))

        here = pl.multiple_of(16 * col, 16)
        keep(source.at[:, pl.ds(here, 16)], target.at[:, pl.ds(here, 16)], phase)
        arrived(target, phase)

    def exchange_z(source, target, phase):
        @pl.loop(1, 16)
        def _(step):
            put(source.at[zi ^ step], target.at[zi], phase, peer_z(step))

        keep(source.at[zi], target.at[zi], phase)
        arrived(target, phase)

    def exchange_x(source, target, phase):
        here = pl.multiple_of(4 * xi, 4)

        @pl.loop(1, 64)
        def _(step):
            there = pl.multiple_of(4 * (xi ^ step), 4)
            put(source.at[pl.ds(there, 4)], target.at[pl.ds(here, 4)], phase, peer_x(step))

        keep(source.at[pl.ds(here, 4)], target.at[pl.ds(here, 4)], phase)
        arrived(target, phase)

    def wave_y(k):
        return (8 * zi + k).astype(F32)

    exchange_y(s1, r1, 1)
    stage_y(r1, s2, wy_h, wy_l)
    exchange_z(s2, r2, 2)
    stage_z(r2, s3, cs_h, cs_l, wave_y)
    exchange_x(s3, r3, 3)
    stage_x(r3, s4, cs_h, cs_l, 8 * zi + (xi & 7), xi >> 3)
    exchange_x(s4, r4, 4)
    stage_z_back(r4, s5, cs_h, cs_l, wave_y)
    exchange_z(s5, r5, 5)
    stage_y_back(r5, s6, vy_h, vy_l)
    exchange_y(s6, r6, 6)
    for j in range(4):
        for d in range(3):
            for quad in range(4):
                at = (2 * quad + j // 2) * 16 + (j % 2) * 8
                cb[j, d, 8 * quad : 8 * quad + 8, :] = r6[d, at : at + 8, :]
    put(cb.at[pl.ds(1 - core, 3)], r7, 7, partner)
    arrived(r7, 7)
    for s in range(SLOTS):
        key = jnp.where(core == 1, 8 - count, 0) + s
        mine = cb[jnp.clip(key - 4 * core, 0, 3)]
        theirs = r7[jnp.clip(jnp.where(core == 1, key - 1, key - 4), 0, 2)]
        used = s < count
        value = jnp.where(used, jnp.where((key >> 2) == core, mine, theirs), 0.0)
        comp[s] = value
        sol[s] = jnp.where(used, vel[s] - value, 0.0)

    left(s0, 0)
    left(s1.at[:, pl.ds(0, 112)], 1)
    left(s2.at[pl.ds(0, 15)], 2)
    left(s3.at[pl.ds(0, 252)], 3)
    left(s4.at[pl.ds(0, 252)], 4)
    left(s5.at[pl.ds(0, 15)], 5)
    left(s6.at[:, pl.ds(0, 112)], 6)
    left(cb.at[pl.ds(0, 3)], 7)


def body(velocity, counts):
    vmem = pl.BlockSpec(memory_space=pltpu.VMEM)
    blocks = velocity.reshape(SLOTS, 3, 32, 128)
    shape = jax.ShapeDtypeStruct((SLOTS, 3, 32, 128), F32)
    tables = [jnp.asarray(table) for table in weights()]
    part = pltpu.VMEM((3, 3, 32, 128), F32)
    fields = pltpu.VMEM((3, 128, 128), F32)
    lines = pltpu.VMEM((16, 24, 128), F32)
    pencils = pltpu.VMEM((N, 128), F32)
    comp, sol = pl.pallas_call(
        kernel,
        out_shape=(shape, shape),
        in_specs=[vmem, pl.BlockSpec(memory_space=pltpu.SMEM)] + [vmem] * 6,
        out_specs=(vmem, vmem),
        scratch_shapes=[
            part, part, fields, fields, lines, lines, pencils, pencils, pencils, pencils, lines, lines, fields, fields,
            pltpu.VMEM((4, 3, 32, 128), F32), part,
            pltpu.SemaphoreType.DMA((8,)), pltpu.SemaphoreType.DMA((8,)),
        ],
        compiler_params=pltpu.CompilerParams(
            collective_id=0, has_side_effects=True, vmem_limit_bytes=32 * 1024 * 1024
        ),
        name="helmholtz",
    )(blocks, counts, *tables)
    return comp.reshape(velocity.shape), sol.reshape(velocity.shape)


def solution(mesh):
    blocks, owners = P("col", "row", None, None, None), P("col", "row")
    return jax.shard_map(body, mesh=mesh, in_specs=(blocks, owners), out_specs=(blocks, blocks), check_vma=False)
```

profile of v0, /device:TPU:1, one launch (start us, length us, event | category | flops | bytes accessed | tf_op | source)
XLA Modules:
  0.0 89.0 jit_solution(8335513126657052138)
XLA Ops:
  1.3 0.0 copy-start
  1.3 1.0 %copy-done = f32[1,1,7,3,4096]{4,1,3,2,0:T(1,128)S(1)} copy-done((f32[1,1,7,3,4096]{4,1,3,2,0:T(1,128)S(1)}, f32[1,1,7,3,4096]{4,1,3,2,0:T(1,128)}, u32[]{:S(2)}) %copy-start) | copy-done | bytes 344088
  2.3 0.0 copy-start.1
  2.3 0.9 %copy-done.1 = bf16[256,512]{1,0:T(8,128)(2,1)S(1)} copy-done((bf16[256,512]{1,0:T(8,128)(2,1)S(1)}, bf16[256,512]{1,0:T(8,128)(2,1)}, u32[]{:S(2)}) %copy-start.1) | copy-done | bytes 262168
  3.2 0.0 copy-start.2
  3.2 0.9 %copy-done.2 = bf16[256,512]{1,0:T(8,128)(2,1)S(1)} copy-done((bf16[256,512]{1,0:T(8,128)(2,1)S(1)}, bf16[256,512]{1,0:T(8,128)(2,1)}, u32[]{:S(2)}) %copy-start.2) | copy-done | bytes 262168
  4.2 0.0 copy-start.3
  4.2 0.9 %copy-done.3 = bf16[256,256]{1,0:T(8,128)(2,1)S(1)} copy-done((bf16[256,256]{1,0:T(8,128)(2,1)S(1)}, bf16[256,256]{1,0:T(8,128)(2,1)}, u32[]{:S(2)}) %copy-start.3) | copy-done | bytes 131096
  5.1 0.0 copy-start.4
  5.1 0.9 %copy-done.4 = bf16[256,256]{1,0:T(8,128)(2,1)S(1)} copy-done((bf16[256,256]{1,0:T(8,128)(2,1)S(1)}, bf16[256,256]{1,0:T(8,128)(2,1)}, u32[]{:S(2)}) %copy-start.4) | copy-done | bytes 131096
  6.0 0.0 copy-start.5
  6.0 0.9 %copy-done.5 = bf16[256,256]{1,0:T(8,128)(2,1)S(1)} copy-done((bf16[256,256]{1,0:T(8,128)(2,1)S(1)}, bf16[256,256]{1,0:T(8,128)(2,1)}, u32[]{:S(2)}) %copy-start.5) | copy-done | bytes 131096
  6.9 0.0 copy-start.6
  6.9 0.9 %copy-done.6 = bf16[256,256]{1,0:T(8,128)(2,1)S(1)} copy-done((bf16[256,256]{1,0:T(8,128)(2,1)S(1)}, bf16[256,256]{1,0:T(8,128)(2,1)}, u32[]{:S(2)}) %copy-start.6) | copy-done | bytes 131096
  7.8 79.7 %helmholtz.1 = (f32[7,3,32,128]{3,2,1,0:T(8,128)S(1)}, f32[7,3,32,128]{3,2,1,0:T(8,128)S(1)}) custom-call(f32[7,3,32,128]{3,2,1,0:T(8,128)S(1)} %bitcast.3, s32[1,1]{1,0:T(1,128)S(6)} %copy.22.cnt, bf16[256,512]{1,0:T(8,128)(2,1)S(1)} %copy-done.2, bf16[256,512]{1,0:T(8,128)(2,1)S(1)} %copy-done.1, bf16[256,256]{1,0:T(8,128)(2,1)S(1)} %copy-done.6, ...), custom_call_target="tpu_custom_call" | custom-call | tf_op jit(solution)/shard_map/helmholtz/pallas_call | solution.py:345
  87.5 0.7 copy.23
  88.2 0.7 copy.24
Async XLA Ops:
  1.3 1.0 %copy-start = (f32[1,1,7,3,4096]{4,1,3,2,0:T(1,128)S(1)}, f32[1,1,7,3,4096]{4,1,3,2,0:T(1,128)}, u32[]{:S(2)}) copy-start(f32[1,1,7,3,4096]{4,1,3,2,0:T(1,128)} %param.8) | copy-start | bytes 1032196
  2.3 0.9 %copy-start.1 = (bf16[256,512]{1,0:T(8,128)(2,1)S(1)}, bf16[256,512]{1,0:T(8,128)(2,1)}, u32[]{:S(2)}) copy-start(bf16[256,512]{1,0:T(8,128)(2,1)} %constant.13.clone.cs_l) | copy-start | bytes 786436
  3.2 0.9 %copy-start.2 = (bf16[256,512]{1,0:T(8,128)(2,1)S(1)}, bf16[256,512]{1,0:T(8,128)(2,1)}, u32[]{:S(2)}) copy-start(bf16[256,512]{1,0:T(8,128)(2,1)} %constant.12.clone.cs_h) | copy-start | bytes 786436
  4.2 0.9 %copy-start.3 = (bf16[256,256]{1,0:T(8,128)(2,1)S(1)}, bf16[256,256]{1,0:T(8,128)(2,1)}, u32[]{:S(2)}) copy-start(bf16[256,256]{1,0:T(8,128)(2,1)} %constant.17.clone.vy_l) | copy-start | bytes 393220
  5.1 0.9 %copy-start.4 = (bf16[256,256]{1,0:T(8,128)(2,1)S(1)}, bf16[256,256]{1,0:T(8,128)(2,1)}, u32[]{:S(2)}) copy-start(bf16[256,256]{1,0:T(8,128)(2,1)} %constant.16.clone.vy_h) | copy-start | bytes 393220
  6.0 0.9 %copy-start.5 = (bf16[256,256]{1,0:T(8,128)(2,1)S(1)}, bf16[256,256]{1,0:T(8,128)(2,1)}, u32[]{:S(2)}) copy-start(bf16[256,256]{1,0:T(8,128)(2,1)} %constant.15.clone.wy_l) | copy-start | bytes 393220
  6.9 0.9 %copy-start.6 = (bf16[256,256]{1,0:T(8,128)(2,1)S(1)}, bf16[256,256]{1,0:T(8,128)(2,1)}, u32[]{:S(2)}) copy-start(bf16[256,256]{1,0:T(8,128)(2,1)} %constant.14.clone.wy_h) | copy-start | bytes 393220
where the time goes:
time: 90.6 us; the launch traced here: 89 us
  Pallas kernels  79.7 us (88%)
  local copies, waits for them, and re-layouts  7.95 us (9%)
  between operations  1.3 us (1%)
    pallas_call x1, Pallas kernels, body(): pl.pallas_call(kernel, out_shape=(shape, shape), in_specs=[vmem, pl.Block...  79.7 us
    unnamed x16, local copies, waits for them, and re-layouts  7.95 us

commit v1 on v0

v1 whole, which is shorter than its diff:
```python
import jax
import jax.numpy as jnp
import ml_dtypes
import numpy as np
from jax import lax
from jax.experimental import pallas as pl
from jax.experimental.pallas import tpu as pltpu
from jax.sharding import PartitionSpec as P

MESH = pl.DeviceIdType.MESH
SLOTS = 7
N = 256
F32 = jnp.float32
BF16 = jnp.bfloat16


def split_np(table):
    head = table.astype(ml_dtypes.bfloat16)
    rest = (table - head.astype(np.float64)).astype(ml_dtypes.bfloat16)
    return head, rest


def weights():
    at = np.arange(N)
    angle = 2 * np.pi * ((at[:, None] * at[None, :]) % N) / N
    cos, sin = np.cos(angle), np.sin(angle)
    high, brick, low = np.meshgrid(np.arange(4), np.arange(16), np.arange(4), indexing="ij")
    x_of = (16 * brick + 4 * high + low).reshape(-1)
    odd, pair = np.meshgrid(np.arange(2), np.arange(64), indexing="ij")
    k_of = (2 * pair + odd).reshape(-1)
    real_rows, imag_rows = cos[:128], -sin[:128].copy()
    imag_rows[0] = cos[128]
    gain = np.full((128, 1), 2.0)
    gain[0] = 1.0
    forward = np.concatenate([real_rows[k_of], imag_rows[k_of]], axis=0)
    back = np.concatenate([(gain * real_rows)[k_of], (gain * imag_rows)[k_of]], axis=0).T
    low, source = np.meshgrid(np.arange(4), np.arange(64), indexing="ij")
    z_of = (4 * source + low).reshape(-1)
    lane = np.arange(N)
    bit = lambda b: (lane >> b) & 1
    y_of = 128 * bit(7) + 64 * bit(3) + 32 * bit(1) + 16 * bit(0) + 8 * bit(2) + ((lane >> 4) & 7)
    both = lambda rows, columns: np.concatenate([t[rows][:, columns] for t in (cos, sin)], axis=1)
    x_both = np.concatenate([forward[:, x_of], back[x_of]], axis=1)
    tables = x_both, both(at, z_of), both(y_of, at), both(at, y_of), both(z_of, at)
    return np.concatenate([part for table in tables for part in split_np(table)], axis=0)


def lane_roll(value, shift):
    return pltpu.roll(value, shift % 128, value.ndim - 1)


def lane_bit(shape, bit):
    return (lax.broadcasted_iota(jnp.int32, shape, len(shape) - 1) // (1 << bit)) % 2 == 1


def swap_bit(low, high, bit):
    upper = lane_bit(low.shape, bit)
    step = 1 << bit
    return jnp.where(upper, lane_roll(high, step), low), jnp.where(upper, high, lane_roll(low, -step))


def swap_bits(items, pairs):
    items = list(items)
    for index_bit, bit in pairs:
        for at in range(len(items)):
            if not (at >> index_bit) & 1:
                other = at | (1 << index_bit)
                items[at], items[other] = swap_bit(items[at], items[other], bit)
    return items


def halves(value):
    head = value.astype(BF16)
    return head, (value - head.astype(F32)).astype(BF16)


def dot(left, right):
    return lax.dot_general(left, right, (((1,), (0,)), ((), ())), preferred_element_type=F32)


def dot_left(table, value):
    head, rest = (part[...] for part in table)
    value_head, value_rest = halves(value)
    return dot(head, value_head) + (dot(head, value_rest) + dot(rest, value_head))


def dot_right(value, table):
    head, rest = (part[...] for part in table)
    value_head, value_rest = halves(value)
    return dot(value_head, head) + (dot(value_rest, head) + dot(value_head, rest))


def signed(index):
    return jnp.where(index == N // 2, 0, jnp.where(index > N // 2, index - N, index)).astype(F32)


def iota(shape, axis):
    return lax.broadcasted_iota(jnp.int32, shape, axis)


def spread(number):
    return (number & 1) + 2 * (number & 2) + 4 * (number & 4) + 8 * (number & 8)


def gathered_bits(number):
    return (number & 1) + ((number >> 1) & 2) + ((number >> 2) & 4) + ((number >> 3) & 8)


def pack(block, s1, j, first):
    items = swap_bits([block[:, 8 * i : 8 * i + 8] for i in range(4)], [(0, 2), (1, 3)])
    for i in range(4):
        at = 8 * (j % 2 + 2 * i + 8 * (j // 2))
        s1[first : first + block.shape[0], at : at + 8, :] = items[i]


def unpack(r6, cb, j, first, count):
    at = [8 * (j % 2 + 2 * i + 8 * (j // 2)) for i in range(4)]
    items = swap_bits([r6[first : first + count, a : a + 8, :] for a in at], [(0, 2), (1, 3)])
    for i in range(4):
        cb[first : first + count, j, 8 * i : 8 * i + 8, :] = items[i]


def stage_x_pair(r1, s2, table):
    items = [r1[d, pl.ds(e, 64, stride=2), :] for d in range(2) for e in range(2)]
    out = dot_left(table, jnp.concatenate(swap_bits(items, [(0, 2), (1, 3)]), axis=0))
    for q in range(4):
        s2[pl.ds(q, 64, stride=4), :] = out[64 * q : 64 * q + 64]


def stage_x_lone(r1, s2, table):
    items = swap_bits([r1[2, pl.ds(e, 64, stride=2), :] for e in range(2)], [(0, 2)])
    upper = lane_bit((64, 128), 3)
    items = [jnp.where(upper, lane_roll(a, 8), a) for a in items] + [jnp.where(upper, a, lane_roll(a, -8)) for a in items]
    out = dot_left(table, jnp.concatenate(items, axis=0))
    for odd in range(2):
        real, imag = (out[64 * q : 64 * q + 64] for q in (odd, 2 + odd))
        s2[pl.ds(odd, 64, stride=2), :] = jnp.where(upper, imag, real)


def turn(value, bit, sign):
    upper, step = lane_bit(value.shape, bit), 1 << bit
    from_low, from_high = lane_roll(value, step), lane_roll(value, -step)
    return jnp.where(upper, -from_low, from_high) if sign > 0 else jnp.where(upper, from_low, -from_high)


def stage_z_lone(r2, table):
    items = swap_bits([r2[pl.ds(odd, 64, stride=2), :] for odd in range(2)], [(0, 0)])
    upper = lane_bit((64, 128), 1)
    items = [jnp.where(upper, lane_roll(a, 2), a) for a in items] + [jnp.where(upper, a, lane_roll(a, -2)) for a in items]
    value = jnp.concatenate(items, axis=0)
    out = dot_left(table, jnp.concatenate([value, turn(value, 3, 1)], axis=0))
    return jnp.where(lane_bit(out.shape, 1), lane_roll(out, -8), out)


def stage_z_pair(r2, s3, lone, table, zi):
    items = swap_bits([r2[pl.ds(q, 64, stride=4), :] for q in range(4)], [(0, 0), (1, 1)])
    value = jnp.concatenate(items, axis=0)
    out = dot_left(table, jnp.concatenate([value, turn(value, 1, 1)], axis=0))
    wave_x = (2 * zi + iota(out.shape, 1) % 2).astype(F32)
    wave_z = signed(iota(out.shape, 0))
    s3[...] = jnp.where(lane_bit(out.shape, 3), out, wave_x * out + wave_z * lone)


def stage_y(r3, s4, ahead, behind, zi, yi):
    def rows(at):
        return slice(16 * at, 16 * at + 16)

    order = [(0, 0), (1, 1), (2, 3)]
    tiles = [swap_bits([r3[rows(8 * high + low), :] for low in range(8)], order) for high in range(2)]
    left = jnp.concatenate([jnp.concatenate([tiles[0][i], tiles[1][i]], axis=1) for i in range(8)], axis=0)
    out = dot_right(left, ahead).reshape(8, 16, 2 * N)
    by_cos, by_sin = out[..., :N], out[..., N:]
    wave_y = signed(iota((16, N), 1))
    wave_z = signed(16 * yi + iota((16, N), 0))
    fields = [None] * 8
    for odd in range(2):
        wave_x = (2 * zi + odd).astype(F32)
        square_sum = jnp.maximum(wave_x * wave_x + wave_y * wave_y + wave_z * wave_z, 1.0)
        real = [by_cos[4 * c + odd] + by_sin[4 * c + 2 + odd] for c in range(2)]
        imag = [by_cos[4 * c + 2 + odd] - by_sin[4 * c + odd] for c in range(2)]
        for i, part in enumerate((real, imag)):
            potential = (part[0] + wave_y * part[1]) / square_sum
            fields[2 * i + odd] = potential
            fields[4 + 2 * i + odd] = wave_y * potential
    out = dot_right(jnp.concatenate(fields, axis=0), behind).reshape(8, 16, 2 * N)
    by_cos, by_sin = out[..., :N], out[..., N:]
    items = [None] * 8
    for c in range(2):
        for odd in range(2):
            real, imag = 4 * c + odd, 4 * c + 2 + odd
            items[real] = by_cos[real] - by_sin[imag]
            items[imag] = by_cos[imag] + by_sin[real]
    for high in range(2):
        tile = swap_bits([item[:, 128 * high : 128 * high + 128] for item in items], order)
        for low in range(8):
            s4[rows(8 * high + low), :] = tile[low]


def stage_z_back_lone(r4, s5, table):
    value = signed(iota((N, 128), 0)) * r4[...]
    out = dot_left(table, jnp.concatenate([value, turn(value, 1, -1)], axis=0))
    out = [out[64 * i : 64 * i + 64] for i in range(4)]
    high, low = lane_bit((64, 128), 3), lane_bit((64, 128), 1)
    items = []
    for i in range(2):
        real = jnp.where(low, lane_roll(out[2 + i], 2), out[i])
        imag = jnp.where(low, lane_roll(out[2 + i], 8), lane_roll(out[i], 6))
        items.append(jnp.where(high, imag, real))
    items = swap_bits(items, [(0, 0)])
    for odd in range(2):
        s5[pl.ds(odd, 64, stride=2), :] = items[odd]


def stage_z_back_pair(r4, s5, table, zi):
    value = r4[...]
    wave_x = (2 * zi + iota(value.shape, 1) % 2).astype(F32)
    value = jnp.where(lane_bit(value.shape, 3), value, wave_x * value)
    out = dot_left(table, jnp.concatenate([value, turn(value, 1, -1)], axis=0))
    items = swap_bits([out[64 * i : 64 * i + 64] for i in range(4)], [(0, 0), (1, 1)])
    for q in range(4):
        s5[pl.ds(q, 64, stride=4), :] = items[q]


def stage_x_back_lone(r5, s6, table):
    value = jnp.concatenate([r5[pl.ds(odd, 64, stride=2), :] for odd in range(2)], axis=0)
    out = dot_left(table, jnp.concatenate([value, lane_roll(value, -8)], axis=0))
    out = [out[64 * i : 64 * i + 64] for i in range(4)]
    upper = lane_bit((64, 128), 3)
    items = swap_bits([jnp.where(upper, lane_roll(out[2 + i], 8), out[i]) for i in range(2)], [(0, 2)])
    for e in range(2):
        s6[2, pl.ds(e, 64, stride=2), :] = items[e]


def stage_x_back_pair(r5, s6, table):
    value = jnp.concatenate([r5[pl.ds(q, 64, stride=4), :] for q in range(4)], axis=0)
    out = dot_left(table, value)
    items = swap_bits([out[64 * i : 64 * i + 64] for i in range(4)], [(0, 2), (1, 3)])
    for d in range(2):
        for e in range(2):
            s6[d, pl.ds(e, 64, stride=2), :] = items[2 * d + e]


PHASES = 14


def kernel(
    vel_hbm, cnt, tables_hbm, value, kept,
    vel, tables, load, s0, r0, s1, r1, s2p, r2p, s2l, r2l, s3, r3, s4, r4, s5p, r5p, s5l, r5l, s6, r6, cb, r7, send, recv,
):
    loads = [pltpu.make_async_copy(vel_hbm, vel, load.at[0])]
    for table in range(5):
        rows = pl.ds(512 * table, 512)
        loads.append(pltpu.make_async_copy(tables_hbm.at[rows], tables.at[rows], load.at[1 + table]))
    loads[0].start()

    def table(at, columns=slice(0, 512)):
        return tables.at[512 * at : 512 * at + 256, columns], tables.at[512 * at + 256 : 512 * at + 512, columns]

    x_ahead, x_behind = table(0, slice(0, 256)), table(0, slice(256, 512))
    z_ahead, y_ahead, y_behind, z_behind = (table(at) for at in range(1, 5))
    row, col = lax.axis_index("row"), lax.axis_index("col")
    core = row & 1
    px, pz = gathered_bits(row), gathered_bits(row >> 1)
    zi = 8 * pz + (px >> 1)
    yi = 2 * col + core

    def peer_x(step):
        return (row ^ spread(step), col)

    def peer_z(step):
        return (row ^ (4 * spread(step & 7) + 2 * spread(step >> 3)), col)

    def peer_y(step):
        return (row ^ (step & 1), col ^ (step >> 1))

    partner = (row ^ 1, col)

    barrier = pltpu.get_barrier_semaphore()
    for peer, count in ((peer_z, 64), (peer_x, 16), (peer_y, 16)):

        @pl.loop(1, count)
        def _(turn_at, peer=peer, count=count):
            pl.semaphore_signal(barrier, inc=1, device_id=peer(count - turn_at), device_id_type=MESH)

    for item in loads[1:]:
        item.start()
    loads[0].wait()

    def put(source, target, phase, device):
        pltpu.make_async_remote_copy(
            src_ref=source, dst_ref=target, send_sem=send.at[phase], recv_sem=recv.at[phase],
            device_id=device, device_id_type=MESH,
        ).start()

    def keep(source, target, phase):
        pltpu.make_async_copy(source, target, recv.at[phase]).start()

    def arrived(buffer, phase):
        pltpu.make_async_copy(buffer, buffer, recv.at[phase]).wait()

    def left(part, phase):
        pltpu.make_async_copy(part, part, send.at[phase]).wait()

    def spread_out(source, target, phase, me, count, width, peer, part=None):
        def at(ref, place):
            rows = pl.ds(pl.multiple_of(width * place, width), width)
            return ref.at[rows] if part is None else ref.at[part, rows]

        @pl.loop(1, count)
        def _(turn_at):
            step = count - turn_at
            put(at(source, me ^ step), at(target, me), phase, peer(step))

        keep(at(source, me), at(target, me), phase)

    lone, pair = pl.ds(2, 1), pl.ds(0, 2)

    count = cnt[0, 0]
    for i in range(3):
        block = vel[jnp.where(core == 1, jnp.maximum(count - 7 + i, 0), 4 + i)]
        for d in range(3):
            s0[d, i] = block[d]
    pl.semaphore_wait(barrier, 63 + 15 + 15)
    put(s0.at[lone], r0.at[lone], 0, partner)
    put(s0.at[pair], r0.at[pair], 1, partner)

    def bricks(first, number):
        for j in range(4):
            slot = jnp.where(core == 1, count - 4 + j, j)
            owned = jnp.where(core == 1, slot >= 0, j < count)
            mine = vel[jnp.clip(slot, 0, SLOTS - 1)][first : first + number]
            at = jnp.clip(jnp.where(core == 1, j, j - 1), 0, 2)
            theirs = jnp.stack([r0[d, at] for d in range(first, first + number)])
            pack(jnp.where(owned, mine, theirs), s1, j, first)

    arrived(r0.at[lone], 0)
    bricks(2, 1)
    spread_out(s1, r1, 2, px, 16, 8, peer_x, lone)
    arrived(r0.at[pair], 1)
    bricks(0, 2)
    spread_out(s1, r1, 3, px, 16, 8, peer_x, pair)
    for s in range(SLOTS):
        kept[s] = jnp.where(s < count, vel[s], 0.0)

    loads[1].wait()
    arrived(r1.at[lone], 2)
    stage_x_lone(r1, s2l, x_ahead)
    spread_out(s2l, r2l, 4, zi, 64, 2, peer_z)
    arrived(r1.at[pair], 3)
    stage_x_pair(r1, s2p, x_ahead)
    spread_out(s2p, r2p, 5, zi, 64, 4, peer_z)

    loads[2].wait()
    arrived(r2l, 4)
    third = stage_z_lone(r2l, z_ahead)
    arrived(r2p, 5)
    stage_z_pair(r2p, s3, third, z_ahead, zi)
    spread_out(s3, r3, 6, yi, 16, 16, peer_y)

    loads[3].wait()
    loads[4].wait()
    arrived(r3, 6)
    stage_y(r3, s4, y_ahead, y_behind, zi, yi)
    spread_out(s4, r4, 7, yi, 16, 16, peer_y)

    loads[5].wait()
    arrived(r4, 7)
    stage_z_back_lone(r4, s5l, z_behind)
    spread_out(s5l, r5l, 8, zi, 64, 2, peer_z)
    stage_z_back_pair(r4, s5p, z_behind, zi)
    spread_out(s5p, r5p, 9, zi, 64, 4, peer_z)

    arrived(r5l, 8)
    stage_x_back_lone(r5l, s6, x_behind)
    spread_out(s6, r6, 10, px, 16, 8, peer_x, lone)
    arrived(r5p, 9)
    stage_x_back_pair(r5p, s6, x_behind)
    spread_out(s6, r6, 11, px, 16, 8, peer_x, pair)

    theirs = pl.ds(1 - core, 3)
    arrived(r6.at[lone], 10)
    for j in range(4):
        unpack(r6, cb, j, 2, 1)
    put(cb.at[lone, theirs], r7.at[lone], 12, partner)
    arrived(r6.at[pair], 11)
    for j in range(4):
        unpack(r6, cb, j, 0, 2)
    put(cb.at[pair, theirs], r7.at[pair], 13, partner)
    arrived(r7.at[lone], 12)
    arrived(r7.at[pair], 13)
    for s in range(SLOTS):
        key = jnp.where(core == 1, 8 - count, 0) + s
        here, there = jnp.clip(key - 4 * core, 0, 3), jnp.clip(jnp.where(core == 1, key - 1, key - 4), 0, 2)
        for d in range(3):
            block = jnp.where((key >> 2) == core, cb[d, here], r7[d, there])
            value[s, d] = jnp.where(s < count, block, 0.0)

    left(s0.at[lone], 0)
    left(s0.at[pair], 1)
    left(s1.at[lone, pl.ds(0, 120)], 2)
    left(s1.at[pair, pl.ds(0, 120)], 3)
    left(s2l.at[pl.ds(0, 126)], 4)
    left(s2p.at[pl.ds(0, 252)], 5)
    left(s3.at[pl.ds(0, 240)], 6)
    left(s4.at[pl.ds(0, 240)], 7)
    left(s5l.at[pl.ds(0, 126)], 8)
    left(s5p.at[pl.ds(0, 252)], 9)
    left(s6.at[lone, pl.ds(0, 120)], 10)
    left(s6.at[pair, pl.ds(0, 120)], 11)
    left(cb.at[lone, pl.ds(0, 3)], 12)
    left(cb.at[pair, pl.ds(0, 3)], 13)


def body(velocity, counts):
    vmem, hbm = pl.BlockSpec(memory_space=pltpu.VMEM), pl.BlockSpec(memory_space=pltpu.HBM)
    blocks = velocity.reshape(SLOTS, 3, 32, 128)
    shape = jax.ShapeDtypeStruct((SLOTS, 3, 32, 128), F32)
    tables = jnp.asarray(weights())
    part = pltpu.VMEM((3, 3, 32, 128), F32)
    fields = pltpu.VMEM((3, 128, 128), F32)
    full, half = pltpu.VMEM((N, 128), F32), pltpu.VMEM((128, 128), F32)
    value, kept = pl.pallas_call(
        kernel,
        out_shape=(shape, shape),
        in_specs=[hbm, pl.BlockSpec(memory_space=pltpu.SMEM), hbm],
        out_specs=(vmem, vmem),
        scratch_shapes=[
            pltpu.VMEM(shape.shape, F32), pltpu.VMEM(tables.shape, BF16), pltpu.SemaphoreType.DMA((6,)),
            part, part, fields, fields, full, full, half, half, full, full, full, full, full, full, half, half, fields,
            fields, pltpu.VMEM((3, 4, 32, 128), F32), part,
            pltpu.SemaphoreType.DMA((PHASES,)), pltpu.SemaphoreType.DMA((PHASES,)),
        ],
        compiler_params=pltpu.CompilerParams(
            collective_id=0, has_side_effects=True, vmem_limit_bytes=53 * 1024 * 1024
        ),
        name="helmholtz",
    )(blocks, counts, tables)
    comp = value * (1.0 / float(N) ** 3)
    sol = kept - comp
    return comp.reshape(velocity.shape), sol.reshape(velocity.shape)


def solution(mesh):
    blocks, owners = P("col", "row", None, None, None), P("col", "row")
    return jax.shard_map(body, mesh=mesh, in_specs=(blocks, owners), out_specs=(blocks, blocks), check_vma=False)
```

time: 90.6 us -> 76.6 us (0.85); the launches traced: 89 us -> 76.5 us
  local copies, waits for them, and re-layouts: 7.95 us -> 0 us
  Pallas kernels: 79.7 us -> 74.3 us
  other arithmetic: 0 us -> 0.91 us
    unnamed x16 -> x0, local copies, waits for them, and re-layouts: 7.95 us -> none
    pallas_call x1, Pallas kernels: 79.7 us -> 74.3 us  [body(): pl.pallas_call(kernel, out_shape=(shape, shape), in_specs=[hbm, pl.BlockS...]
    sub x0 -> x1, other arithmetic: none -> 0.91 us  [body(): sol = kept - comp]
where the time goes in v1:
time: 76.6 us; the launch traced here: 76.5 us
  Pallas kernels  74.3 us (97%)
  between operations  1.28 us (2%)
  other arithmetic  0.91 us (1%)
    pallas_call x1, Pallas kernels, body(): pl.pallas_call(kernel, out_shape=(shape, shape), in_specs=[hbm, pl.BlockS...  74.3 us

profile of v1, /device:TPU:1, one launch (start us, length us, event | category | flops | bytes accessed | tf_op | source)
XLA Modules:
  0.0 76.5 jit_solution(17826993356879065324)
XLA Ops:
  1.3 74.3 %helmholtz.1 = (f32[7,3,32,128]{3,2,1,0:T(8,128)S(1)}, f32[7,3,32,128]{3,2,1,0:T(8,128)S(1)}) custom-call(f32[7,3,32,128]{3,2,1,0:T(8,128)} %bitcast.3, s32[1,1]{1,0:T(1,128)S(6)} %copy.15.cnt, bf16[2560,512]{1,0:T(8,128)(2,1)} %constant.4.clone.tables_hbm), custom_call_target="tpu_custom_call" | custom-call | tf_op jit(solution)/shard_map/helmholtz/pallas_call | solution.py:422
  75.5 0.9 %fusion = (f32[7,3,32,128]{3,2,1,0:T(8,128)}, f32[7,3,32,128]{3,2,1,0:T(8,128)}) fusion(f32[7,3,32,128]{3,2,1,0:T(8,128)S(1)} %get-tuple-element.5, f32[7,3,32,128]{3,2,1,0:T(8,128)S(1)} %get-tuple-element.4), kind=kLoop, calls=%fused_computation.1 | loop fusion | flops 172032 | bytes 1376256 | tf_op jit(solution)/shard_map/sub | solution.py:439

commit v2 on v1

--- a/solution.py
+++ b/solution.py
@@ -50,7 +50,7 @@
 
 
 def lane_bit(shape, bit):
-    return (lax.broadcasted_iota(jnp.int32, shape, len(shape) - 1) // (1 << bit)) % 2 == 1
+    return (lax.broadcasted_iota(jnp.int32, shape, len(shape) - 1) & (1 << bit)) != 0
 
 
 def swap_bit(low, high, bit):
@@ -79,15 +79,16 @@
 
 
 def dot_left(table, value):
-    head, rest = (part[...] for part in table)
     value_head, value_rest = halves(value)
-    return dot(head, value_head) + (dot(head, value_rest) + dot(rest, value_head))
+    first = dot(table[...], value_head)
+    return first[:N] + (dot(table[:N, :], value_rest) + first[N:])
 
 
 def dot_right(value, table):
-    head, rest = (part[...] for part in table)
+    rows = value.shape[0]
     value_head, value_rest = halves(value)
-    return dot(value_head, head) + (dot(value_rest, head) + dot(value_head, rest))
+    first = dot(jnp.concatenate([value_head, value_rest], axis=0), table[:N, :])
+    return first[:rows] + (first[rows:] + dot(value_head, table[N:, :]))
 
 
 def signed(index):
@@ -156,33 +157,31 @@
     items = swap_bits([r2[pl.ds(q, 64, stride=4), :] for q in range(4)], [(0, 0), (1, 1)])
     value = jnp.concatenate(items, axis=0)
     out = dot_left(table, jnp.concatenate([value, turn(value, 1, 1)], axis=0))
-    wave_x = (2 * zi + iota(out.shape, 1) % 2).astype(F32)
+    wave_x = (2 * zi + (iota(out.shape, 1) & 1)).astype(F32)
     wave_z = signed(iota(out.shape, 0))
-    s3[...] = jnp.where(lane_bit(out.shape, 3), out, wave_x * out + wave_z * lone)
-
-
-def stage_y(r3, s4, ahead, behind, zi, yi):
-    def rows(at):
-        return slice(16 * at, 16 * at + 16)
-
+    s3[...] = jnp.where(lane_bit(out.shape, 3), out, wave_x * out + wave_z * lone).reshape(16, 16, 128)
+
+
+def stage_y(r3, s4, ahead, behind, zi, yi, part):
+    rows = slice(8 * part, 8 * part + 8)
     order = [(0, 0), (1, 1), (2, 3)]
-    tiles = [swap_bits([r3[rows(8 * high + low), :] for low in range(8)], order) for high in range(2)]
+    tiles = [swap_bits([r3[8 * high + low, rows, :] for low in range(8)], order) for high in range(2)]
     left = jnp.concatenate([jnp.concatenate([tiles[0][i], tiles[1][i]], axis=1) for i in range(8)], axis=0)
-    out = dot_right(left, ahead).reshape(8, 16, 2 * N)
+    out = dot_right(left, ahead).reshape(8, 8, 2 * N)
     by_cos, by_sin = out[..., :N], out[..., N:]
-    wave_y = signed(iota((16, N), 1))
-    wave_z = signed(16 * yi + iota((16, N), 0))
+    wave_y = signed(iota((8, N), 1))
+    wave_z = signed(16 * yi + 8 * part + iota((8, N), 0))
     fields = [None] * 8
     for odd in range(2):
         wave_x = (2 * zi + odd).astype(F32)
-        square_sum = jnp.maximum(wave_x * wave_x + wave_y * wave_y + wave_z * wave_z, 1.0)
+        inverse = 1.0 / jnp.maximum(wave_x * wave_x + wave_y * wave_y + wave_z * wave_z, 1.0)
         real = [by_cos[4 * c + odd] + by_sin[4 * c + 2 + odd] for c in range(2)]
         imag = [by_cos[4 * c + 2 + odd] - by_sin[4 * c + odd] for c in range(2)]
         for i, part in enumerate((real, imag)):
-            potential = (part[0] + wave_y * part[1]) / square_sum
+            potential = (part[0] + wave_y * part[1]) * inverse
             fields[2 * i + odd] = potential
             fields[4 + 2 * i + odd] = wave_y * potential
-    out = dot_right(jnp.concatenate(fields, axis=0), behind).reshape(8, 16, 2 * N)
+    out = dot_right(jnp.concatenate(fields, axis=0), behind).reshape(8, 8, 2 * N)
     by_cos, by_sin = out[..., :N], out[..., N:]
     items = [None] * 8
     for c in range(2):
@@ -193,13 +192,17 @@
     for high in range(2):
         tile = swap_bits([item[:, 128 * high : 128 * high + 128] for item in items], order)
         for low in range(8):
-            s4[rows(8 * high + low), :] = tile[low]
-
-
-def stage_z_back_lone(r4, s5, table):
-    value = signed(iota((N, 128), 0)) * r4[...]
-    out = dot_left(table, jnp.concatenate([value, turn(value, 1, -1)], axis=0))
-    out = [out[64 * i : 64 * i + 64] for i in range(4)]
+            s4[8 * high + low, rows, :] = tile[low]
+
+
+def stage_z_back(r4, s5p, s5l, table, zi):
+    value = r4[...].reshape(N, 128)
+    wave_x = (2 * zi + (iota(value.shape, 1) & 1)).astype(F32)
+    third = signed(iota(value.shape, 0)) * value
+    value = jnp.where(lane_bit(value.shape, 3), value, wave_x * value)
+    both = [jnp.concatenate([part, turn(part, 1, -1)], axis=0) for part in (third, value)]
+    both = dot_left(table, jnp.concatenate(both, axis=1))
+    out = [both[64 * i : 64 * i + 64, :128] for i in range(4)]
     high, low = lane_bit((64, 128), 3), lane_bit((64, 128), 1)
     items = []
     for i in range(2):
@@ -208,17 +211,10 @@
         items.append(jnp.where(high, imag, real))
     items = swap_bits(items, [(0, 0)])
     for odd in range(2):
-        s5[pl.ds(odd, 64, stride=2), :] = items[odd]
-
-
-def stage_z_back_pair(r4, s5, table, zi):
-    value = r4[...]
-    wave_x = (2 * zi + iota(value.shape, 1) % 2).astype(F32)
-    value = jnp.where(lane_bit(value.shape, 3), value, wave_x * value)
-    out = dot_left(table, jnp.concatenate([value, turn(value, 1, -1)], axis=0))
-    items = swap_bits([out[64 * i : 64 * i + 64] for i in range(4)], [(0, 0), (1, 1)])
+        s5l[pl.ds(odd, 64, stride=2), :] = items[odd]
+    items = swap_bits([both[64 * i : 64 * i + 64, 128:] for i in range(4)], [(0, 0), (1, 1)])
     for q in range(4):
-        s5[pl.ds(q, 64, stride=4), :] = items[q]
+        s5p[pl.ds(q, 64, stride=4), :] = items[q]
 
 
 def stage_x_back_lone(r5, s6, table):
@@ -240,12 +236,12 @@
             s6[d, pl.ds(e, 64, stride=2), :] = items[2 * d + e]
 
 
-PHASES = 14
+PHASES = 16
 
 
 def kernel(
     vel_hbm, cnt, tables_hbm, value, kept,
-    vel, tables, load, s0, r0, s1, r1, s2p, r2p, s2l, r2l, s3, r3, s4, r4, s5p, r5p, s5l, r5l, s6, r6, cb, r7, send, recv,
+    vel, tables, load, s0, r0, s1, r1, s2p, r2p, s2l, r2l, s3, r3, s4, r4, s5p, r5p, s5l, r5l, s6, r6, cb, r7, send, recv, ready,
 ):
     loads = [pltpu.make_async_copy(vel_hbm, vel, load.at[0])]
     for table in range(5):
@@ -254,7 +250,7 @@
     loads[0].start()
 
     def table(at, columns=slice(0, 512)):
-        return tables.at[512 * at : 512 * at + 256, columns], tables.at[512 * at + 256 : 512 * at + 512, columns]
+        return tables.at[512 * at : 512 * at + 512, columns]
 
     x_ahead, x_behind = table(0, slice(0, 256)), table(0, slice(256, 512))
     z_ahead, y_ahead, y_behind, z_behind = (table(at) for at in range(1, 5))
@@ -270,13 +266,16 @@
     def peer_z(step):
         return (row ^ (4 * spread(step & 7) + 2 * spread(step >> 3)), col)
 
+    def peer_brick(step):
+        return (row ^ (2 * spread(step)), col)
+
     def peer_y(step):
         return (row ^ (step & 1), col ^ (step >> 1))
 
     partner = (row ^ 1, col)
 
     barrier = pltpu.get_barrier_semaphore()
-    for peer, count in ((peer_z, 64), (peer_x, 16), (peer_y, 16)):
+    for peer, count in ((peer_x, 16), (peer_brick, 8), (peer_y, 16)):
 
         @pl.loop(1, count)
         def _(turn_at, peer=peer, count=count):
@@ -313,6 +312,16 @@
 
         keep(at(source, me), at(target, me), phase)
 
+    def spread_y(source, target, phase, part):
+        rows = pl.ds(8 * part, 8)
+
+        @pl.loop(1, 16)
+        def _(turn_at):
+            step = 16 - turn_at
+            put(source.at[yi ^ step, rows], target.at[yi, rows], phase, peer_y(step))
+
+        keep(source.at[yi, rows], target.at[yi, rows], phase)
+
     lone, pair = pl.ds(2, 1), pl.ds(0, 2)
 
     count = cnt[0, 0]
@@ -320,9 +329,13 @@
         block = vel[jnp.where(core == 1, jnp.maximum(count - 7 + i, 0), 4 + i)]
         for d in range(3):
             s0[d, i] = block[d]
-    pl.semaphore_wait(barrier, 63 + 15 + 15)
+    pl.semaphore_wait(barrier, 15 + 7 + 15)
     put(s0.at[lone], r0.at[lone], 0, partner)
     put(s0.at[pair], r0.at[pair], 1, partner)
+
+    @pl.loop(1, 8)
+    def _(turn_at):
+        pl.semaphore_signal(ready, inc=1, device_id=peer_brick(8 - turn_at), device_id_type=MESH)
 
     def bricks(first, number):
         for j in range(4):
@@ -345,6 +358,7 @@
     loads[1].wait()
     arrived(r1.at[lone], 2)
     stage_x_lone(r1, s2l, x_ahead)
+    pl.semaphore_wait(ready, 7)
     spread_out(s2l, r2l, 4, zi, 64, 2, peer_z)
     arrived(r1.at[pair], 3)
     stage_x_pair(r1, s2p, x_ahead)
@@ -355,37 +369,39 @@
     third = stage_z_lone(r2l, z_ahead)
     arrived(r2p, 5)
     stage_z_pair(r2p, s3, third, z_ahead, zi)
-    spread_out(s3, r3, 6, yi, 16, 16, peer_y)
+    spread_y(s3, r3, 6, 0)
+    spread_y(s3, r3, 14, 1)
 
     loads[3].wait()
     loads[4].wait()
-    arrived(r3, 6)
-    stage_y(r3, s4, y_ahead, y_behind, zi, yi)
-    spread_out(s4, r4, 7, yi, 16, 16, peer_y)
+    for part in range(2):
+        arrived(r3.at[:, pl.ds(8 * part, 8)], 6 + 8 * part)
+        stage_y(r3, s4, y_ahead, y_behind, zi, yi, part)
+        spread_y(s4, r4, 7 + 8 * part, part)
 
     loads[5].wait()
-    arrived(r4, 7)
-    stage_z_back_lone(r4, s5l, z_behind)
+    arrived(r4.at[:, pl.ds(0, 8)], 7)
+    arrived(r4.at[:, pl.ds(8, 8)], 15)
+    stage_z_back(r4, s5p, s5l, z_behind, zi)
+    spread_out(s5p, r5p, 9, zi, 64, 4, peer_z)
     spread_out(s5l, r5l, 8, zi, 64, 2, peer_z)
-    stage_z_back_pair(r4, s5p, z_behind, zi)
-    spread_out(s5p, r5p, 9, zi, 64, 4, peer_z)
-
+
+    arrived(r5p, 9)
+    stage_x_back_pair(r5p, s6, x_behind)
+    spread_out(s6, r6, 11, px, 16, 8, peer_x, pair)
     arrived(r5l, 8)
     stage_x_back_lone(r5l, s6, x_behind)
     spread_out(s6, r6, 10, px, 16, 8, peer_x, lone)
-    arrived(r5p, 9)
-    stage_x_back_pair(r5p, s6, x_behind)
-    spread_out(s6, r6, 11, px, 16, 8, peer_x, pair)
 
     theirs = pl.ds(1 - core, 3)
+    arrived(r6.at[pair], 11)
+    for j in range(4):
+        unpack(r6, cb, j, 0, 2)
+    put(cb.at[pair, theirs], r7.at[pair], 13, partner)
     arrived(r6.at[lone], 10)
     for j in range(4):
         unpack(r6, cb, j, 2, 1)
     put(cb.at[lone, theirs], r7.at[lone], 12, partner)
-    arrived(r6.at[pair], 11)
-    for j in range(4):
-        unpack(r6, cb, j, 0, 2)
-    put(cb.at[pair, theirs], r7.at[pair], 13, partner)
     arrived(r7.at[lone], 12)
     arrived(r7.at[pair], 13)
     for s in range(SLOTS):
@@ -401,8 +417,9 @@
     left(s1.at[pair, pl.ds(0, 120)], 3)
     left(s2l.at[pl.ds(0, 126)], 4)
     left(s2p.at[pl.ds(0, 252)], 5)
-    left(s3.at[pl.ds(0, 240)], 6)
-    left(s4.at[pl.ds(0, 240)], 7)
+    for part in range(2):
+        left(s3.at[pl.ds(0, 15), pl.ds(8 * part, 8)], 6 + 8 * part)
+        left(s4.at[pl.ds(0, 15), pl.ds(8 * part, 8)], 7 + 8 * part)
     left(s5l.at[pl.ds(0, 126)], 8)
     left(s5p.at[pl.ds(0, 252)], 9)
     left(s6.at[lone, pl.ds(0, 120)], 10)
@@ -419,6 +436,7 @@
     part = pltpu.VMEM((3, 3, 32, 128), F32)
     fields = pltpu.VMEM((3, 128, 128), F32)
     full, half = pltpu.VMEM((N, 128), F32), pltpu.VMEM((128, 128), F32)
+    rows_y = pltpu.VMEM((16, 16, 128), F32)
     value, kept = pl.pallas_call(
         kernel,
         out_shape=(shape, shape),
@@ -426,9 +444,9 @@
         out_specs=(vmem, vmem),
         scratch_shapes=[
             pltpu.VMEM(shape.shape, F32), pltpu.VMEM(tables.shape, BF16), pltpu.SemaphoreType.DMA((6,)),
-            part, part, fields, fields, full, full, half, half, full, full, full, full, full, full, half, half, fields,
-            fields, pltpu.VMEM((3, 4, 32, 128), F32), part,
-            pltpu.SemaphoreType.DMA((PHASES,)), pltpu.SemaphoreType.DMA((PHASES,)),
+            part, part, fields, fields, full, full, half, half, rows_y, rows_y, rows_y, rows_y, full, full, half, half,
+            fields, fields, pltpu.VMEM((3, 4, 32, 128), F32), part,
+            pltpu.SemaphoreType.DMA((PHASES,)), pltpu.SemaphoreType.DMA((PHASES,)), pltpu.SemaphoreType.REGULAR,
         ],
         compiler_params=pltpu.CompilerParams(
             collective_id=0, has_side_effects=True, vmem_limit_bytes=53 * 1024 * 1024

time: 76.6 us -> 75.1 us (0.980)
  Pallas kernels: 74.3 us -> 72.7 us
    pallas_call x1, Pallas kernels: 74.3 us -> 72.7 us  [body(): pl.pallas_call(kernel, out_shape=(shape, shape), in_specs=[hbm, pl.BlockS...]
where the time goes in v2:
time: 75.1 us; the launch traced here: 74.9 us
  Pallas kernels  72.7 us (97%)
  between operations  1.28 us (2%)
  other arithmetic  0.91 us (1%)
    pallas_call x1, Pallas kernels, body(): pl.pallas_call(kernel, out_shape=(shape, shape), in_specs=[hbm, pl.BlockS...  72.7 us

profile of v2, /device:TPU:1, one launch (start us, length us, event | category | flops | bytes accessed | tf_op | source)
XLA Modules:
  0.0 74.9 jit_solution(5008654001040540213)
XLA Ops:
  1.3 72.7 %helmholtz.1 = (f32[7,3,32,128]{3,2,1,0:T(8,128)S(1)}, f32[7,3,32,128]{3,2,1,0:T(8,128)S(1)}) custom-call(f32[7,3,32,128]{3,2,1,0:T(8,128)} %bitcast.3, s32[1,1]{1,0:T(1,128)S(6)} %copy.15.cnt, bf16[2560,512]{1,0:T(8,128)(2,1)} %constant.4.clone.tables_hbm), custom_call_target="tpu_custom_call" | custom-call | tf_op jit(solution)/shard_map/helmholtz/pallas_call | solution.py:440
  74.0 0.9 %fusion = (f32[7,3,32,128]{3,2,1,0:T(8,128)}, f32[7,3,32,128]{3,2,1,0:T(8,128)}) fusion(f32[7,3,32,128]{3,2,1,0:T(8,128)S(1)} %get-tuple-element.5, f32[7,3,32,128]{3,2,1,0:T(8,128)S(1)} %get-tuple-element.4), kind=kLoop, calls=%fused_computation.1 | loop fusion | flops 172032 | bytes 1376256 | tf_op jit(solution)/shard_map/sub | solution.py:457
